TPU v7x, 32 devices: a whole 2x2x4 slice. The times are simulated.
32 devices in a mesh: row: 16 (over z, y, x), col: 2 (over core).
Axes of the slice: x: 2, y: 2, z: 4, core: 2. Of those that a mesh axis runs over, the one named last changes fastest.
Arguments:
- features: float32 [64, 32768], P(None, ('row', 'col')), may hold values from -12 to 12
- initial: float32 [32768], P(('row', 'col')), may hold values from 0.1 to 90, as said below
Outputs:
- dist: float32 [32768], P(('row', 'col'))
- residuals: float32 [2], replicated
Inputs may be any that keep to these rules, and one draw needn't show every extreme that they name: `initial`: positive starting weights of the policies.
All inputs are finite; a program needn't handle non-finite values.
Results may differ from a plain program's by a relative error of at most 0.0003.
Values sent between devices are 32-bit elements; how exact they have to be, the bound alone decides.
A program may use at most 64 MiB of HBM per device.

v0:
```python
import functools

import jax
import jax.numpy as jnp
from jax import lax
from jax.experimental import pallas as pl
from jax.experimental.pallas import tpu as pltpu
from jax.sharding import PartitionSpec as P

intensity = 0.25
ROW_TILE = 256
MESH_ID = pl.DeviceIdType.MESH
f32, bf16 = jnp.float32, jnp.bfloat16


def split3(x):
    hi = x.astype(bf16).astype(f32)
    mid = (x - hi).astype(bf16).astype(f32)
    return hi, mid, (x - hi - mid).astype(bf16).astype(f32)


def weight_rows(w, count):
    shape = (count, w.shape[1])
    hi, mid, low = (jnp.broadcast_to(v, shape) for v in split3(w))
    at = lax.broadcasted_iota(jnp.int32, shape, 0)
    tail = jnp.where(at == 3, 1.0, 0.0).astype(f32)
    return jnp.where(at == 0, hi, jnp.where(at == 1, mid, jnp.where(at == 2, low, tail)))


def kernel(
    A, B, feat_ref, init_ref, dist_ref, res_ref,
    col_feat, row_feat, col_w, row_w, col_in, row_in, col_out, row_out, grown,
    row_op, col_op, left, right, kept, row_acc, col_acc, scal,
    send_sem, recv_sem, scal_send, scal_recv,
):
    half = feat_ref.shape[0] // 2
    n = feat_ref.shape[1]
    devices = 2 * A * B
    total = n * devices
    row, core = lax.axis_index("row"), lax.axis_index("col")
    me = row * 2 + core
    p, q = lax.div(row, B), lax.rem(row, B)
    tile = min(ROW_TILE, n)
    own = A

    def later(x, y):
        return jnp.where(x > y, 1, 0)

    row_partner = [None] + [(p * B + (q ^ d), core) for d in range(1, B)]
    col_user = [(row, 1 - core)]
    col_owner = [(row, 1 - core)]
    for d in range(1, A):
        other = p ^ d
        col_user.append((other * B + q, core ^ later(p, other)))
        col_owner.append((other * B + q, core ^ later(other, p)))

    def exchange(round_id, row_src, row_dst, col_src, col_dst, col_to):
        copies = {}
        for d in range(max(A, B)):
            for is_row in (False, True):
                if d >= (B if is_row else A) or (is_row and d == 0):
                    continue
                slot = A + d if is_row else d
                copies[is_row, d] = pltpu.make_async_remote_copy(
                    src_ref=row_src(d) if is_row else col_src(d),
                    dst_ref=row_dst(d) if is_row else col_dst(d),
                    send_sem=send_sem.at[round_id, slot],
                    recv_sem=recv_sem.at[round_id, slot],
                    device_id=row_partner[d] if is_row else col_to[d],
                    device_id_type=MESH_ID,
                )
                copies[is_row, d].start()
        return copies

    def scal_copy(round_id, other, slot):
        return pltpu.make_async_remote_copy(
            src_ref=scal.at[round_id, me],
            dst_ref=scal.at[round_id, slot],
            send_sem=scal_send.at[round_id, other],
            recv_sem=scal_recv.at[round_id, slot],
            device_id=(lax.div(other, 2), lax.rem(other, 2)),
            device_id_type=MESH_ID,
        )

    def scal_start(round_id, value):
        scal[round_id, me] = value

        def one(k, carry):
            scal_copy(round_id, lax.rem(me + k, devices), me).start()
            return carry

        lax.fori_loop(1, devices, one, 0)

    def scal_finish(round_id):
        def one(k, carry):
            other = lax.rem(me + k, devices)
            scal_copy(round_id, other, other).wait()
            return carry

        lax.fori_loop(1, devices, one, 0)
        return jnp.sum(scal[round_id], axis=0)

    def lanes(x):
        return jnp.broadcast_to(jnp.sum(x, axis=1, keepdims=True), (1, 128))

    barrier = pltpu.get_barrier_semaphore()

    def greet(k, carry):
        other = lax.rem(me + k, devices)
        pl.semaphore_signal(
            barrier, inc=1, device_id=(lax.div(other, 2), lax.rem(other, 2)), device_id_type=MESH_ID
        )
        return carry

    lax.fori_loop(1, devices, greet, 0)
    pl.semaphore_wait(barrier, devices - 1)

    feats = exchange(
        0, lambda d: feat_ref, lambda d: row_feat.at[d], lambda d: feat_ref, lambda d: col_feat.at[d], col_user
    )
    starts = exchange(
        1, lambda d: init_ref, lambda d: row_w.at[0, d], lambda d: init_ref, lambda d: col_w.at[0, d], col_user
    )
    weights0 = init_ref[...]
    scal_start(0, lanes(weights0))

    row_acc[...] = jnp.zeros_like(row_acc)
    col_acc[...] = jnp.zeros_like(col_acc)

    def prepare_row(slot, f):
        g = jnp.concatenate([f[half:], -f[:half]], axis=0) * (0.5 * intensity)
        hi = g.astype(bf16).astype(f32)
        both = jnp.concatenate([hi, g - hi], axis=0)
        x = both.T.astype(bf16)
        row_op[slot] = jnp.concatenate([x, x], axis=1)

    def prepare_col(slot, f):
        hi = f.astype(bf16)
        low = (f - hi.astype(f32)).astype(bf16)
        col_op[slot] = jnp.concatenate([hi, hi, low, low], axis=0)

    def weigh_row(slot, w):
        left[slot] = weight_rows(w, 16).astype(bf16)

    def weigh_col(slot, w):
        right[slot] = weight_rows(w, 128).T.astype(bf16)

    def unit(first, kept_slot, row_slot, col_slot, scale):
        down = jnp.zeros((16, n), f32)
        for r in range(n // tile):
            at = pl.ds(r * tile, tile)
            if first:
                payoff = jnp.dot(row_op[row_slot, at], col_op[col_slot], preferred_element_type=f32)
                t = jnp.tanh(payoff).astype(bf16)
                kept[kept_slot, at] = t
            else:
                t = kept[kept_slot, at]
            across = jnp.dot(t, right[col_slot], preferred_element_type=f32)
            row_acc[row_slot, at] += scale * across
            down += jnp.dot(left[row_slot, :, r * tile:(r + 1) * tile], t, preferred_element_type=f32)
        col_acc[col_slot] += scale * down

    def units(first, arrive):
        def shell(m, carry):
            arrive(m)

            def one(j, carry):
                dq = jnp.where(j <= m, m, j - m - 1)
                dp = jnp.where(j <= m, j, m)
                own_or_sibling = jnp.where((q ^ dq) > q, 0, own)
                col_slot = jnp.where(dp == 0, own_or_sibling, dp)
                scale = jnp.where(dq + dp == 0, 0.5, 1.0).astype(f32)

                def run():
                    unit(first, dq * A + dp, dq, col_slot, scale)

                if A == B:
                    run()
                else:
                    pl.when((dq < B) & (dp < A))(run)
                return carry

            return lax.fori_loop(0, 2 * m + 1, one, carry)

        lax.fori_loop(0, max(A, B), shell, 0)

    def sibling_unit(first):
        unit(first, A * B, 0, 0, f32(0.5))

    def wait_slot(copies_sem_round, is_row, d, src, dst):
        slot = A + d if is_row else d
        return pltpu.make_async_remote_copy(
            src_ref=src, dst_ref=dst, send_sem=send_sem.at[copies_sem_round, slot],
            recv_sem=recv_sem.at[copies_sem_round, slot], device_id=(row, 1 - core), device_id_type=MESH_ID,
        )

    prepare_row(0, feat_ref[...])
    prepare_col(own, feat_ref[...])
    weigh_row(0, weights0)
    weigh_col(own, weights0)

    def arrive_first(m):
        @pl.when(m < A)
        def _():
            wait_slot(0, False, m, feat_ref, col_feat.at[m]).wait()
            wait_slot(1, False, m, init_ref, col_w.at[0, m]).wait()
            prepare_col(m, col_feat[m])
            weigh_col(m, col_w[0, m])

        @pl.when((m < B) & (m > 0))
        def _():
            wait_slot(0, True, m, feat_ref, row_feat.at[m]).wait()
            wait_slot(1, True, m, init_ref, row_w.at[0, m]).wait()
            prepare_row(m, row_feat[m])
            weigh_row(m, row_w[0, m])

    units(True, arrive_first)
    sibling_unit(True)

    def partials(it):
        def of_row(acc):
            a = acc.T
            return -(a[0:1] + a[1:2] + a[2:3]), a[3:4]

        def of_col(acc):
            return acc[0:1] + acc[1:2] + acc[2:3], -acc[3:4]

        everything = jnp.zeros((1, n), f32)
        for d in range(1, B):
            y, t = of_row(row_acc[d])
            row_out[it, d] = jnp.concatenate([y, t], axis=0)
            everything += y
        for d in range(A):
            y, t = of_col(col_acc[d])
            col_out[it, d] = jnp.concatenate([y, t], axis=0)
            everything += y
        y0, t0 = of_row(row_acc[0])
        y1, t1 = of_col(col_acc[own])
        mine = jnp.concatenate([y0 + y1, t0 + t1], axis=0)
        return mine, everything + y0 + y1

    def send_partials(it):
        return exchange(
            2 + 2 * it,
            lambda d: row_out.at[it, d], lambda d: row_in.at[it, d],
            lambda d: col_out.at[it, d], lambda d: col_in.at[it, d], col_owner,
        )

    def receive(it, copies, mine):
        for (is_row, d), copy in copies.items():
            copy.wait()
            mine = mine + (row_in[it, d] if is_row else col_in[it, d])
        return mine

    def wide(x):
        return jnp.broadcast_to(x[:, 0:1], (1, n))

    step_rate = 1.0 / total
    mine, _ = partials(0)
    copies = send_partials(0)
    sum0 = wide(scal_finish(0))
    mine = receive(0, copies, mine)
    y, t = mine[0:1], mine[1:2]
    stay = 1.0 - step_rate * (0.5 * total + 0.5 * t)
    grown0 = step_rate * (0.5 * sum0 + 0.5 * y) + weights0 * stay
    grown[...] = grown0
    seconds = exchange(
        3, lambda d: grown, lambda d: row_w.at[1, d], lambda d: grown, lambda d: col_w.at[1, d], col_user
    )
    scal_start(1, lanes(grown0))

    row_acc[...] = jnp.zeros_like(row_acc)
    col_acc[...] = jnp.zeros_like(col_acc)
    weigh_row(0, grown0)
    weigh_col(own, grown0)

    def arrive_second(m):
        @pl.when(m < A)
        def _():
            wait_slot(3, False, m, grown, col_w.at[1, m]).wait()
            weigh_col(m, col_w[1, m])

        @pl.when((m < B) & (m > 0))
        def _():
            wait_slot(3, True, m, grown, row_w.at[1, m]).wait()
            weigh_row(m, row_w[1, m])

    units(False, arrive_second)
    sibling_unit(False)

    sum1 = wide(scal_finish(1))
    mine, everything = partials(1)
    copies = send_partials(1)
    base = step_rate * (0.5 * sum1) + grown0 * stay
    scal_start(2, lanes(base + (0.5 * step_rate) * everything))
    first_change = lanes(jnp.abs(grown0 / sum1 - weights0 / sum0))
    mine = receive(1, copies, mine)
    grown1 = base + (0.5 * step_rate) * mine[0:1]
    sum2 = wide(scal_finish(2))
    final = grown1 / sum2
    second_change = lanes(jnp.abs(final - grown0 / sum1))
    lane = lax.broadcasted_iota(jnp.int32, (1, 128), 1)
    scal_start(3, jnp.where(lane == 0, first_change, second_change))
    dist_ref[...] = total * final
    res_ref[...] = scal_finish(3)


def on_device(A, B, features, initial):
    feats, n = features.shape
    devices = 2 * A * B
    vmem = lambda *shape: pltpu.VMEM(shape, f32)
    dist, res = pl.pallas_call(
        functools.partial(kernel, A, B),
        out_shape=(jax.ShapeDtypeStruct((1, n), f32), jax.ShapeDtypeStruct((1, 128), f32)),
        in_specs=[pl.BlockSpec(memory_space=pltpu.VMEM)] * 2,
        out_specs=(pl.BlockSpec(memory_space=pltpu.VMEM),) * 2,
        scratch_shapes=[
            vmem(A, feats, n), vmem(B, feats, n), vmem(2, A, 1, n), vmem(2, B, 1, n),
            vmem(2, A, 2, n), vmem(2, B, 2, n), vmem(2, A, 2, n), vmem(2, B, 2, n), vmem(1, n),
            pltpu.VMEM((B, n, 4 * feats), bf16), pltpu.VMEM((A + 1, 4 * feats, n), bf16),
            pltpu.VMEM((B, 16, n), bf16), pltpu.VMEM((A + 1, n, 128), bf16),
            pltpu.VMEM((A * B + 1, n, n), bf16),
            vmem(B, n, 128), vmem(A + 1, 16, n), vmem(4, devices, 1, 128),
            pltpu.SemaphoreType.DMA((5, A + B)), pltpu.SemaphoreType.DMA((5, A + B)),
            pltpu.SemaphoreType.DMA((4, devices)), pltpu.SemaphoreType.DMA((4, devices)),
        ],
        compiler_params=pltpu.CompilerParams(
            collective_id=0, has_side_effects=True, vmem_limit_bytes=56 * 1024 * 1024
        ),
    )(features, initial.reshape(1, n))
    return dist.reshape(n), res[0, :2]


def solution(mesh):
    rows = mesh.shape["row"]
    B = 1
    while 4 * B * B <= rows:
        B *= 2
    A = rows // B
    placed = (P(None, ("row", "col")), P(("row", "col")))
    return jax.shard_map(
        functools.partial(on_device, A, B), mesh=mesh, in_specs=placed,
        out_specs=(P(("row", "col")), P()), check_vma=False,
    )
```

profile of v0, /device:TPU:0, one launch (start us, length us, event | category | flops | bytes accessed | tf_op | source)
XLA Modules:
  0.0 92.4 jit_solution(11144486524764352195)
XLA Ops:
  0.6 90.0 %shard_map.41 = (f32[1,1024]{1,0:T(1,128)}, f32[1,128]{1,0:T(1,128)}) custom-call(f32[64,1024]{1,0:T(8,128)} %feat_ref.1, f32[1,1024]{1,0:T(1,128)} %bitcast.4), custom_call_target="tpu_custom_call" | custom-call | tf_op jit(solution)/shard_map/pallas_call | solution.py:312
  90.7 0.0 copy-start
  90.7 0.0 copy-start.1
  90.7 0.6 copy-done.1
  91.3 0.5 slice_bitcast_fusion
  91.8 0.0 copy-done
  91.8 0.6 copy.5
Async XLA Ops:
  90.7 1.2 %copy-start = (f32[1,1024]{1,0:T(1,128)S(1)}, f32[1,1024]{1,0:T(1,128)}, u32[]{:S(2)}) copy-start(f32[1,1024]{1,0:T(1,128)} %get-tuple-element.4) | copy-start | bytes 12292
  90.7 0.6 copy-start.1
where the time goes:
time: 92.6 us; the launch traced here: 92.4 us
  Pallas kernels  90 us (97%)
  local copies, waits for them, and re-layouts  1.74 us (2%)
    pallas_call x1, Pallas kernels, on_device(): pl.pallas_call(functools.partial(kernel, A, B), out_shape=(jax.ShapeDtype...  90 us

commit v1 on v0

--- a/solution.py
+++ b/solution.py
@@ -143,24 +143,46 @@
         left[slot] = weight_rows(w, 16).astype(bf16)
 
     def weigh_col(slot, w):
-        right[slot] = weight_rows(w, 128).T.astype(bf16)
+        right[slot] = w
 
     def unit(first, kept_slot, row_slot, col_slot, scale):
         down = jnp.zeros((16, n), f32)
+        across_w = jnp.broadcast_to(right[col_slot], (8, n))
         for r in range(n // tile):
             at = pl.ds(r * tile, tile)
             if first:
                 payoff = jnp.dot(row_op[row_slot, at], col_op[col_slot], preferred_element_type=f32)
-                t = jnp.tanh(payoff).astype(bf16)
+                wide_t = jnp.tanh(payoff)
+                t = wide_t.astype(bf16)
                 kept[kept_slot, at] = t
             else:
                 t = kept[kept_slot, at]
-            across = jnp.dot(t, right[col_slot], preferred_element_type=f32)
-            row_acc[row_slot, at] += scale * across
+                wide_t = t.astype(f32)
+            weighed = jnp.zeros((tile, 128), f32)
+            plain = jnp.zeros((tile, 128), f32)
+            for k in range(n // 128):
+                part = wide_t[:, k * 128:(k + 1) * 128]
+                by = across_w[:, k * 128:(k + 1) * 128]
+                weighed += (part.reshape(tile // 8, 8, 128) * by[None]).reshape(tile, 128)
+                if first:
+                    plain += part
+            row_acc[0, row_slot, at] += weighed if scale is None else scale * weighed
+            if first:
+                row_acc[1, row_slot, at] += plain if scale is None else scale * plain
             down += jnp.dot(left[row_slot, :, r * tile:(r + 1) * tile], t, preferred_element_type=f32)
-        col_acc[col_slot] += scale * down
+        col_acc[col_slot] += down if scale is None else scale * down
 
     def units(first, arrive):
+        def near(j, carry):
+            @pl.when(j == 1)
+            def _():
+                arrive(0)
+
+            unit(first, jnp.where(j == 0, 0, A * B), 0, jnp.where(j == 0, own, 0), 0.5)
+            return carry
+
+        lax.fori_loop(0, 2, near, 0)
+
         def shell(m, carry):
             arrive(m)
 
@@ -169,10 +191,9 @@
                 dp = jnp.where(j <= m, j, m)
                 own_or_sibling = jnp.where((q ^ dq) > q, 0, own)
                 col_slot = jnp.where(dp == 0, own_or_sibling, dp)
-                scale = jnp.where(dq + dp == 0, 0.5, 1.0).astype(f32)
 
                 def run():
-                    unit(first, dq * A + dp, dq, col_slot, scale)
+                    unit(first, dq * A + dp, dq, col_slot, None)
 
                 if A == B:
                     run()
@@ -182,10 +203,7 @@
 
             return lax.fori_loop(0, 2 * m + 1, one, carry)
 
-        lax.fori_loop(0, max(A, B), shell, 0)
-
-    def sibling_unit(first):
-        unit(first, A * B, 0, 0, f32(0.5))
+        lax.fori_loop(1, max(A, B), shell, 0)
 
     def wait_slot(copies_sem_round, is_row, d, src, dst):
         slot = A + d if is_row else d
@@ -215,26 +233,26 @@
             weigh_row(m, row_w[0, m])
 
     units(True, arrive_first)
-    sibling_unit(True)
 
     def partials(it):
-        def of_row(acc):
-            a = acc.T
-            return -(a[0:1] + a[1:2] + a[2:3]), a[3:4]
+        def of_row(d):
+            y = jnp.sum(row_acc[0, d].T, axis=0, keepdims=True)
+            t = jnp.sum(row_acc[1, d].T, axis=0, keepdims=True) if it == 0 else jnp.zeros((1, n), f32)
+            return -y, t
 
         def of_col(acc):
             return acc[0:1] + acc[1:2] + acc[2:3], -acc[3:4]
 
         everything = jnp.zeros((1, n), f32)
         for d in range(1, B):
-            y, t = of_row(row_acc[d])
+            y, t = of_row(d)
             row_out[it, d] = jnp.concatenate([y, t], axis=0)
             everything += y
         for d in range(A):
             y, t = of_col(col_acc[d])
             col_out[it, d] = jnp.concatenate([y, t], axis=0)
             everything += y
-        y0, t0 = of_row(row_acc[0])
+        y0, t0 = of_row(0)
         y1, t1 = of_col(col_acc[own])
         mine = jnp.concatenate([y0 + y1, t0 + t1], axis=0)
         return mine, everything + y0 + y1
@@ -286,7 +304,6 @@
             weigh_row(m, row_w[1, m])
 
     units(False, arrive_second)
-    sibling_unit(False)
 
     sum1 = wide(scal_finish(1))
     mine, everything = partials(1)
@@ -301,8 +318,10 @@
     second_change = lanes(jnp.abs(final - grown0 / sum1))
     lane = lax.broadcasted_iota(jnp.int32, (1, 128), 1)
     scal_start(3, jnp.where(lane == 0, first_change, second_change))
-    dist_ref[...] = total * final
-    res_ref[...] = scal_finish(3)
+    dist_ref[...] = (total * final).reshape(n)
+    both = scal_finish(3)
+    res_ref[0] = jnp.sum(jnp.where(lane == 0, both, 0.0))
+    res_ref[1] = jnp.sum(jnp.where(lane == 1, both, 0.0))
 
 
 def on_device(A, B, features, initial):
@@ -311,16 +330,16 @@
     vmem = lambda *shape: pltpu.VMEM(shape, f32)
     dist, res = pl.pallas_call(
         functools.partial(kernel, A, B),
-        out_shape=(jax.ShapeDtypeStruct((1, n), f32), jax.ShapeDtypeStruct((1, 128), f32)),
+        out_shape=(jax.ShapeDtypeStruct((n,), f32), jax.ShapeDtypeStruct((2,), f32)),
         in_specs=[pl.BlockSpec(memory_space=pltpu.VMEM)] * 2,
-        out_specs=(pl.BlockSpec(memory_space=pltpu.VMEM),) * 2,
+        out_specs=(pl.BlockSpec(memory_space=pltpu.VMEM), pl.BlockSpec(memory_space=pltpu.SMEM)),
         scratch_shapes=[
             vmem(A, feats, n), vmem(B, feats, n), vmem(2, A, 1, n), vmem(2, B, 1, n),
             vmem(2, A, 2, n), vmem(2, B, 2, n), vmem(2, A, 2, n), vmem(2, B, 2, n), vmem(1, n),
             pltpu.VMEM((B, n, 4 * feats), bf16), pltpu.VMEM((A + 1, 4 * feats, n), bf16),
-            pltpu.VMEM((B, 16, n), bf16), pltpu.VMEM((A + 1, n, 128), bf16),
+            pltpu.VMEM((B, 16, n), bf16), vmem(A + 1, 1, n),
             pltpu.VMEM((A * B + 1, n, n), bf16),
-            vmem(B, n, 128), vmem(A + 1, 16, n), vmem(4, devices, 1, 128),
+            vmem(2, B, n, 128), vmem(A + 1, 16, n), vmem(4, devices, 1, 128),
             pltpu.SemaphoreType.DMA((5, A + B)), pltpu.SemaphoreType.DMA((5, A + B)),
             pltpu.SemaphoreType.DMA((4, devices)), pltpu.SemaphoreType.DMA((4, devices)),
         ],
@@ -328,7 +347,7 @@
             collective_id=0, has_side_effects=True, vmem_limit_bytes=56 * 1024 * 1024
         ),
     )(features, initial.reshape(1, n))
-    return dist.reshape(n), res[0, :2]
+    return dist, res
 
 
 def solution(mesh):

time: 92.6 us -> 84.5 us (0.913)
  Pallas kernels: 90 us -> 82 us
    pallas_call x1, Pallas kernels: 90 us -> 82 us  [on_device(): pl.pallas_call(functools.partial(kernel, A, B), out_shape=(jax.ShapeDtype...]
where the time goes in v1:
time: 84.5 us; the launch traced here: 84.4 us
  Pallas kernels  82 us (97%)
  local copies, waits for them, and re-layouts  1.78 us (2%)
    pallas_call x1, Pallas kernels, on_device(): pl.pallas_call(functools.partial(kernel, A, B), out_shape=(jax.ShapeDtype...  82 us
    unnamed x4, local copies, waits for them, and re-layouts  1.78 us

profile of v1, /device:TPU:0, one launch (start us, length us, event | category | flops | bytes accessed | tf_op | source)
XLA Modules:
  0.0 84.4 jit_solution(8221100221987163471)
XLA Ops:
  0.6 82.0 %shard_map.41 = (f32[1024]{0:T(1024)}, f32[2]{0:T(128)}) custom-call(f32[64,1024]{1,0:T(8,128)} %feat_ref.1, f32[1,1024]{1,0:T(1,128)} %bitcast.1), custom_call_target="tpu_custom_call" | custom-call | tf_op jit(solution)/shard_map/pallas_call | solution.py:331
  82.6 0.0 copy-start
  82.6 1.3 %copy.6 = f32[1024]{0:T(1024)} copy(f32[1024]{0:T(1024)} %get-tuple-element.4) | data formatting | bytes 8192
  83.9 0.0 copy-done
  83.9 0.5 copy.7
Async XLA Ops:
  82.6 1.3 %copy-start = (f32[2]{0:T(128)S(1)}, f32[2]{0:T(128)}, u32[]{:S(2)}) copy-start(f32[2]{0:T(128)} %get-tuple-element.5) | copy-start | bytes 28

commit v2 on v1

--- a/solution.py
+++ b/solution.py
@@ -47,30 +47,49 @@
         return jnp.where(x > y, 1, 0)
 
     row_partner = [None] + [(p * B + (q ^ d), core) for d in range(1, B)]
-    col_user = [(row, 1 - core)]
-    col_owner = [(row, 1 - core)]
-    for d in range(1, A):
-        other = p ^ d
-        col_user.append((other * B + q, core ^ later(p, other)))
-        col_owner.append((other * B + q, core ^ later(other, p)))
-
-    def exchange(round_id, row_src, row_dst, col_src, col_dst, col_to):
-        copies = {}
-        for d in range(max(A, B)):
-            for is_row in (False, True):
-                if d >= (B if is_row else A) or (is_row and d == 0):
-                    continue
-                slot = A + d if is_row else d
-                copies[is_row, d] = pltpu.make_async_remote_copy(
-                    src_ref=row_src(d) if is_row else col_src(d),
-                    dst_ref=row_dst(d) if is_row else col_dst(d),
-                    send_sem=send_sem.at[round_id, slot],
-                    recv_sem=recv_sem.at[round_id, slot],
-                    device_id=row_partner[d] if is_row else col_to[d],
-                    device_id_type=MESH_ID,
-                )
-                copies[is_row, d].start()
-        return copies
+    others = [p] + [lax.rem(p + d, A) for d in range(1, A)]
+    col_user = [(row, 1 - core)] + [(o * B + q, core ^ later(p, o)) for o in others[1:]]
+    col_owner = [(row, 1 - core)] + [(o * B + q, core ^ later(o, p)) for o in others[1:]]
+
+    def copy_to(round_id, src, dst, send_slot, recv_slot, device):
+        return pltpu.make_async_remote_copy(
+            src_ref=src, dst_ref=dst, send_sem=send_sem.at[round_id, send_slot],
+            recv_sem=recv_sem.at[round_id, recv_slot], device_id=device, device_id_type=MESH_ID,
+        )
+
+    def row_copies(round_id, src, dst):
+        return [
+            copy_to(round_id, src(d), dst.at[d], A + d, A + d, row_partner[d]) for d in range(1, B)
+        ]
+
+    def col_copies(round_id, src, dst, to):
+        return [copy_to(round_id, src(d), dst.at[p], d, p, to[d]) for d in range(A)]
+
+    def landed(round_id, dst, slot, sem_slot):
+        copy_to(round_id, dst.at[slot], dst.at[slot], sem_slot, sem_slot, (row, 1 - core)).wait_recv()
+
+    can_up, can_down = p < A - 1, p > 0
+    up, down_at = ((p + 1) * B + q, core), ((p - 1) * B + q, core)
+    own_up = copy_to(0, feat_ref, col_feat.at[p], A + B, p, up)
+    own_down = copy_to(0, feat_ref, col_feat.at[p], A + B + 1, p, ((p - 1) * B + q, 1 - core))
+    to_sibling = copy_to(0, feat_ref, col_feat.at[p], p, p, (row, 1 - core))
+
+    def pass_on(o, act):
+        @pl.when((o < p) & can_up)
+        def _():
+            act(copy_to(0, col_feat.at[o], col_feat.at[o], o, o, up))
+
+        @pl.when((o > p) & can_down)
+        def _():
+            act(copy_to(0, col_feat.at[o], col_feat.at[o], o, o, down_at))
+
+    def at_distance(m):
+        above = A - 1 - p
+        near = jnp.minimum(p, above)
+        step = lax.div(m + 1, 2)
+        mixed = jnp.where(lax.rem(m, 2) == 1, p - step, p + step)
+        rest = jnp.where(above > p, p + m - near, p - m + near)
+        return jnp.where(m <= 2 * near, mixed, rest)
 
     def scal_copy(round_id, other, slot):
         return pltpu.make_async_remote_copy(
@@ -115,12 +134,21 @@
     lax.fori_loop(1, devices, greet, 0)
     pl.semaphore_wait(barrier, devices - 1)
 
-    feats = exchange(
-        0, lambda d: feat_ref, lambda d: row_feat.at[d], lambda d: feat_ref, lambda d: col_feat.at[d], col_user
-    )
-    starts = exchange(
-        1, lambda d: init_ref, lambda d: row_w.at[0, d], lambda d: init_ref, lambda d: col_w.at[0, d], col_user
-    )
+    to_sibling.start()
+
+    @pl.when(can_up)
+    def _():
+        own_up.start()
+
+    @pl.when(can_down)
+    def _():
+        own_down.start()
+
+    feat_rows = row_copies(0, lambda d: feat_ref, row_feat)
+    start_rows = row_copies(1, lambda d: init_ref, row_w.at[0])
+    start_cols = col_copies(1, lambda d: init_ref, col_w.at[0], col_user)
+    for copy in feat_rows + start_rows + start_cols:
+        copy.start()
     weights0 = init_ref[...]
     scal_start(0, lanes(weights0))
 
@@ -172,25 +200,34 @@
             down += jnp.dot(left[row_slot, :, r * tile:(r + 1) * tile], t, preferred_element_type=f32)
         col_acc[col_slot] += down if scale is None else scale * down
 
-    def units(first, arrive):
+    def units(first, land, arrive):
         def near(j, carry):
             @pl.when(j == 1)
             def _():
+                land(0)
                 arrive(0)
 
-            unit(first, jnp.where(j == 0, 0, A * B), 0, jnp.where(j == 0, own, 0), 0.5)
+            unit(first, jnp.where(j == 0, 0, A * B), 0, jnp.where(j == 0, own, p), 0.5)
             return carry
 
         lax.fori_loop(0, 2, near, 0)
 
         def shell(m, carry):
+            @pl.when((m == 1) | jnp.logical_not(can_up & can_down))
+            def _():
+                land(m)
+
             arrive(m)
 
             def one(j, carry):
                 dq = jnp.where(j <= m, m, j - m - 1)
                 dp = jnp.where(j <= m, j, m)
-                own_or_sibling = jnp.where((q ^ dq) > q, 0, own)
-                col_slot = jnp.where(dp == 0, own_or_sibling, dp)
+                own_or_sibling = jnp.where((q ^ dq) > q, p, own)
+                col_slot = jnp.where(dp == 0, own_or_sibling, at_distance(jnp.maximum(dp, 1)))
+
+                @pl.when((j == m) & (m < max(A, B) - 1) & can_up & can_down)
+                def _():
+                    land(m + 1)
 
                 def run():
                     unit(first, dq * A + dp, dq, col_slot, None)
@@ -205,34 +242,37 @@
 
         lax.fori_loop(1, max(A, B), shell, 0)
 
-    def wait_slot(copies_sem_round, is_row, d, src, dst):
-        slot = A + d if is_row else d
-        return pltpu.make_async_remote_copy(
-            src_ref=src, dst_ref=dst, send_sem=send_sem.at[copies_sem_round, slot],
-            recv_sem=recv_sem.at[copies_sem_round, slot], device_id=(row, 1 - core), device_id_type=MESH_ID,
-        )
-
     prepare_row(0, feat_ref[...])
     prepare_col(own, feat_ref[...])
     weigh_row(0, weights0)
     weigh_col(own, weights0)
 
+    def place(m):
+        return jnp.where(m == 0, p, at_distance(jnp.maximum(m, 1)))
+
+    def land_first(m):
+        @pl.when(m < A)
+        def _():
+            o = place(m)
+            landed(0, col_feat, o, o)
+            pass_on(o, lambda copy: copy.start())
+
     def arrive_first(m):
         @pl.when(m < A)
         def _():
-            wait_slot(0, False, m, feat_ref, col_feat.at[m]).wait()
-            wait_slot(1, False, m, init_ref, col_w.at[0, m]).wait()
-            prepare_col(m, col_feat[m])
-            weigh_col(m, col_w[0, m])
+            o = place(m)
+            landed(1, col_w.at[0], o, o)
+            prepare_col(o, col_feat[o])
+            weigh_col(o, col_w[0, o])
 
         @pl.when((m < B) & (m > 0))
         def _():
-            wait_slot(0, True, m, feat_ref, row_feat.at[m]).wait()
-            wait_slot(1, True, m, init_ref, row_w.at[0, m]).wait()
+            landed(0, row_feat, m, A + m)
+            landed(1, row_w.at[0], m, A + m)
             prepare_row(m, row_feat[m])
             weigh_row(m, row_w[0, m])
 
-    units(True, arrive_first)
+    units(True, land_first, arrive_first)
 
     def partials(it):
         def of_row(d):
@@ -249,7 +289,7 @@
             row_out[it, d] = jnp.concatenate([y, t], axis=0)
             everything += y
         for d in range(A):
-            y, t = of_col(col_acc[d])
+            y, t = of_col(col_acc[others[d]])
             col_out[it, d] = jnp.concatenate([y, t], axis=0)
             everything += y
         y0, t0 = of_row(0)
@@ -258,16 +298,19 @@
         return mine, everything + y0 + y1
 
     def send_partials(it):
-        return exchange(
-            2 + 2 * it,
-            lambda d: row_out.at[it, d], lambda d: row_in.at[it, d],
-            lambda d: col_out.at[it, d], lambda d: col_in.at[it, d], col_owner,
-        )
-
-    def receive(it, copies, mine):
-        for (is_row, d), copy in copies.items():
-            copy.wait()
-            mine = mine + (row_in[it, d] if is_row else col_in[it, d])
+        copies = row_copies(2 + 2 * it, lambda d: row_out.at[it, d], row_in.at[it])
+        copies += col_copies(2 + 2 * it, lambda d: col_out.at[it, d], col_in.at[it], col_owner)
+        for copy in copies:
+            copy.start()
+        return copies
+
+    def receive(it, mine):
+        for d in range(1, B):
+            landed(2 + 2 * it, row_in.at[it], d, A + d)
+            mine = mine + row_in[it, d]
+        for d in range(A):
+            landed(2 + 2 * it, col_in.at[it], d, d)
+            mine = mine + col_in[it, d]
         return mine
 
     def wide(x):
@@ -275,16 +318,16 @@
 
     step_rate = 1.0 / total
     mine, _ = partials(0)
-    copies = send_partials(0)
+    sent = send_partials(0)
     sum0 = wide(scal_finish(0))
-    mine = receive(0, copies, mine)
+    mine = receive(0, mine)
     y, t = mine[0:1], mine[1:2]
     stay = 1.0 - step_rate * (0.5 * total + 0.5 * t)
     grown0 = step_rate * (0.5 * sum0 + 0.5 * y) + weights0 * stay
     grown[...] = grown0
-    seconds = exchange(
-        3, lambda d: grown, lambda d: row_w.at[1, d], lambda d: grown, lambda d: col_w.at[1, d], col_user
-    )
+    seconds = row_copies(3, lambda d: grown, row_w.at[1]) + col_copies(3, lambda d: grown, col_w.at[1], col_user)
+    for copy in seconds:
+        copy.start()
     scal_start(1, lanes(grown0))
 
     row_acc[...] = jnp.zeros_like(row_acc)
@@ -295,23 +338,24 @@
     def arrive_second(m):
         @pl.when(m < A)
         def _():
-            wait_slot(3, False, m, grown, col_w.at[1, m]).wait()
-            weigh_col(m, col_w[1, m])
+            o = place(m)
+            landed(3, col_w.at[1], o, o)
+            weigh_col(o, col_w[1, o])
 
         @pl.when((m < B) & (m > 0))
         def _():
-            wait_slot(3, True, m, grown, row_w.at[1, m]).wait()
+            landed(3, row_w.at[1], m, A + m)
             weigh_row(m, row_w[1, m])
 
-    units(False, arrive_second)
+    units(False, lambda m: None, arrive_second)
 
     sum1 = wide(scal_finish(1))
     mine, everything = partials(1)
-    copies = send_partials(1)
+    sent += send_partials(1)
     base = step_rate * (0.5 * sum1) + grown0 * stay
     scal_start(2, lanes(base + (0.5 * step_rate) * everything))
     first_change = lanes(jnp.abs(grown0 / sum1 - weights0 / sum0))
-    mine = receive(1, copies, mine)
+    mine = receive(1, mine)
     grown1 = base + (0.5 * step_rate) * mine[0:1]
     sum2 = wide(scal_finish(2))
     final = grown1 / sum2
@@ -322,6 +366,20 @@
     both = scal_finish(3)
     res_ref[0] = jnp.sum(jnp.where(lane == 0, both, 0.0))
     res_ref[1] = jnp.sum(jnp.where(lane == 1, both, 0.0))
+
+    for copy in feat_rows + start_rows + start_cols + seconds + sent + [to_sibling]:
+        copy.wait_send()
+
+    @pl.when(can_up)
+    def _():
+        own_up.wait_send()
+
+    @pl.when(can_down)
+    def _():
+        own_down.wait_send()
+
+    for o in others[1:]:
+        pass_on(o, lambda copy: copy.wait_send())
 
 
 def on_device(A, B, features, initial):
@@ -340,7 +398,7 @@
             pltpu.VMEM((B, 16, n), bf16), vmem(A + 1, 1, n),
             pltpu.VMEM((A * B + 1, n, n), bf16),
             vmem(2, B, n, 128), vmem(A + 1, 16, n), vmem(4, devices, 1, 128),
-            pltpu.SemaphoreType.DMA((5, A + B)), pltpu.SemaphoreType.DMA((5, A + B)),
+            pltpu.SemaphoreType.DMA((5, A + B + 2)), pltpu.SemaphoreType.DMA((5, A + B)),
             pltpu.SemaphoreType.DMA((4, devices)), pltpu.SemaphoreType.DMA((4, devices)),
         ],
         compiler_params=pltpu.CompilerParams(

time: 84.5 us -> 80.6 us (0.954)
  Pallas kernels: 82 us -> 78 us
    pallas_call x1, Pallas kernels: 82 us -> 78 us  [on_device(): pl.pallas_call(functools.partial(kernel, A, B), out_shape=(jax.ShapeDtype...]
where the time goes in v2:
time: 80.6 us; the launch traced here: 80.4 us
  Pallas kernels  78 us (97%)
  local copies, waits for them, and re-layouts  1.78 us (2%)
    pallas_call x1, Pallas kernels, on_device(): pl.pallas_call(functools.partial(kernel, A, B), out_shape=(jax.ShapeDtype...  78 us
    unnamed x4, local copies, waits for them, and re-layouts  1.78 us

profile of v2, /device:TPU:0, one launch (start us, length us, event | category | flops | bytes accessed | tf_op | source)
XLA Modules:
  0.0 80.4 jit_solution(11699631282064194462)
XLA Ops:
  0.6 78.0 %shard_map.41 = (f32[1024]{0:T(1024)}, f32[2]{0:T(128)}) custom-call(f32[64,1024]{1,0:T(8,128)} %feat_ref.1, f32[1,1024]{1,0:T(1,128)} %bitcast.1), custom_call_target="tpu_custom_call" | custom-call | tf_op jit(solution)/shard_map/pallas_call | solution.py:389
  78.6 0.0 copy-start
  78.6 1.3 %copy.6 = f32[1024]{0:T(1024)} copy(f32[1024]{0:T(1024)} %get-tuple-element.4) | data formatting | bytes 8192
  79.9 0.0 copy-done
  79.9 0.5 copy.7
Async XLA Ops:
  78.6 1.3 %copy-start = (f32[2]{0:T(128)S(1)}, f32[2]{0:T(128)}, u32[]{:S(2)}) copy-start(f32[2]{0:T(128)} %get-tuple-element.5) | copy-start | bytes 28

commit v3 on v2

--- a/solution.py
+++ b/solution.py
@@ -91,69 +91,36 @@
         rest = jnp.where(above > p, p + m - near, p - m + near)
         return jnp.where(m <= 2 * near, mixed, rest)
 
-    def scal_copy(round_id, other, slot):
-        return pltpu.make_async_remote_copy(
-            src_ref=scal.at[round_id, me],
-            dst_ref=scal.at[round_id, slot],
-            send_sem=scal_send.at[round_id, other],
-            recv_sem=scal_recv.at[round_id, slot],
-            device_id=(lax.div(other, 2), lax.rem(other, 2)),
-            device_id_type=MESH_ID,
-        )
+    def all_others(act):
+        if devices <= 64:
+            for k in range(1, devices):
+                act((row ^ (k // 2), core ^ (k % 2)))
+        else:
+            def one(k, carry):
+                act((row ^ lax.div(k, 2), core ^ lax.rem(k, 2)))
+                return carry
+
+            lax.fori_loop(1, devices, one, 0)
 
     def scal_start(round_id, value):
         scal[round_id, me] = value
-
-        def one(k, carry):
-            scal_copy(round_id, lax.rem(me + k, devices), me).start()
-            return carry
-
-        lax.fori_loop(1, devices, one, 0)
+        all_others(lambda device: pltpu.make_async_remote_copy(
+            src_ref=scal.at[round_id, me], dst_ref=scal.at[round_id, me], send_sem=scal_send.at[round_id],
+            recv_sem=scal_recv.at[round_id], device_id=device, device_id_type=MESH_ID,
+        ).start())
 
     def scal_finish(round_id):
-        def one(k, carry):
-            other = lax.rem(me + k, devices)
-            scal_copy(round_id, other, other).wait()
-            return carry
-
-        lax.fori_loop(1, devices, one, 0)
+        every = scal.at[round_id, pl.ds(0, devices - 1)]
+        copy = pltpu.make_async_remote_copy(
+            src_ref=every, dst_ref=every, send_sem=scal_send.at[round_id],
+            recv_sem=scal_recv.at[round_id], device_id=(row, 1 - core), device_id_type=MESH_ID,
+        )
+        copy.wait_recv()
+        copy.wait_send()
         return jnp.sum(scal[round_id], axis=0)
 
     def lanes(x):
         return jnp.broadcast_to(jnp.sum(x, axis=1, keepdims=True), (1, 128))
-
-    barrier = pltpu.get_barrier_semaphore()
-
-    def greet(k, carry):
-        other = lax.rem(me + k, devices)
-        pl.semaphore_signal(
-            barrier, inc=1, device_id=(lax.div(other, 2), lax.rem(other, 2)), device_id_type=MESH_ID
-        )
-        return carry
-
-    lax.fori_loop(1, devices, greet, 0)
-    pl.semaphore_wait(barrier, devices - 1)
-
-    to_sibling.start()
-
-    @pl.when(can_up)
-    def _():
-        own_up.start()
-
-    @pl.when(can_down)
-    def _():
-        own_down.start()
-
-    feat_rows = row_copies(0, lambda d: feat_ref, row_feat)
-    start_rows = row_copies(1, lambda d: init_ref, row_w.at[0])
-    start_cols = col_copies(1, lambda d: init_ref, col_w.at[0], col_user)
-    for copy in feat_rows + start_rows + start_cols:
-        copy.start()
-    weights0 = init_ref[...]
-    scal_start(0, lanes(weights0))
-
-    row_acc[...] = jnp.zeros_like(row_acc)
-    col_acc[...] = jnp.zeros_like(col_acc)
 
     def prepare_row(slot, f):
         g = jnp.concatenate([f[half:], -f[:half]], axis=0) * (0.5 * intensity)
@@ -173,6 +140,36 @@
     def weigh_col(slot, w):
         right[slot] = w
 
+    barrier = pltpu.get_barrier_semaphore()
+
+    all_others(lambda device: pl.semaphore_signal(
+        barrier, inc=1, device_id=device, device_id_type=MESH_ID
+    ))
+
+    weights0 = init_ref[...]
+    row_acc[...] = jnp.zeros_like(row_acc)
+    col_acc[...] = jnp.zeros_like(col_acc)
+    prepare_row(0, feat_ref[...])
+    prepare_col(own, feat_ref[...])
+    weigh_row(0, weights0)
+    weigh_col(own, weights0)
+    pl.semaphore_wait(barrier, devices - 1)
+
+    to_sibling.start()
+
+    @pl.when(can_up)
+    def _():
+        own_up.start()
+
+    @pl.when(can_down)
+    def _():
+        own_down.start()
+
+    feat_rows = row_copies(0, lambda d: feat_ref, row_feat)
+    start_rows = row_copies(1, lambda d: init_ref, row_w.at[0])
+    start_cols = col_copies(1, lambda d: init_ref, col_w.at[0], col_user)
+    for copy in feat_rows + start_rows + start_cols:
+        copy.start()
     def unit(first, kept_slot, row_slot, col_slot, scale):
         down = jnp.zeros((16, n), f32)
         across_w = jnp.broadcast_to(right[col_slot], (8, n))
@@ -200,7 +197,7 @@
             down += jnp.dot(left[row_slot, :, r * tile:(r + 1) * tile], t, preferred_element_type=f32)
         col_acc[col_slot] += down if scale is None else scale * down
 
-    def units(first, land, arrive):
+    def units(first, land, arrive, between):
         def near(j, carry):
             @pl.when(j == 1)
             def _():
@@ -211,6 +208,7 @@
             return carry
 
         lax.fori_loop(0, 2, near, 0)
+        between()
 
         def shell(m, carry):
             @pl.when((m == 1) | jnp.logical_not(can_up & can_down))
@@ -242,10 +240,6 @@
 
         lax.fori_loop(1, max(A, B), shell, 0)
 
-    prepare_row(0, feat_ref[...])
-    prepare_col(own, feat_ref[...])
-    weigh_row(0, weights0)
-    weigh_col(own, weights0)
 
     def place(m):
         return jnp.where(m == 0, p, at_distance(jnp.maximum(m, 1)))
@@ -272,7 +266,7 @@
             prepare_row(m, row_feat[m])
             weigh_row(m, row_w[0, m])
 
-    units(True, land_first, arrive_first)
+    units(True, land_first, arrive_first, lambda: scal_start(0, lanes(weights0)))
 
     def partials(it):
         def of_row(d):
@@ -328,9 +322,8 @@
     seconds = row_copies(3, lambda d: grown, row_w.at[1]) + col_copies(3, lambda d: grown, col_w.at[1], col_user)
     for copy in seconds:
         copy.start()
-    scal_start(1, lanes(grown0))
-
-    row_acc[...] = jnp.zeros_like(row_acc)
+
+    row_acc[0] = jnp.zeros((B, n, 128), f32)
     col_acc[...] = jnp.zeros_like(col_acc)
     weigh_row(0, grown0)
     weigh_col(own, grown0)
@@ -347,7 +340,7 @@
             landed(3, row_w.at[1], m, A + m)
             weigh_row(m, row_w[1, m])
 
-    units(False, lambda m: None, arrive_second)
+    units(False, lambda m: None, arrive_second, lambda: scal_start(1, lanes(grown0)))
 
     sum1 = wide(scal_finish(1))
     mine, everything = partials(1)
@@ -399,7 +392,7 @@
             pltpu.VMEM((A * B + 1, n, n), bf16),
             vmem(2, B, n, 128), vmem(A + 1, 16, n), vmem(4, devices, 1, 128),
             pltpu.SemaphoreType.DMA((5, A + B + 2)), pltpu.SemaphoreType.DMA((5, A + B)),
-            pltpu.SemaphoreType.DMA((4, devices)), pltpu.SemaphoreType.DMA((4, devices)),
+            pltpu.SemaphoreType.DMA((4,)), pltpu.SemaphoreType.DMA((4,)),
         ],
         compiler_params=pltpu.CompilerParams(
             collective_id=0, has_side_effects=True, vmem_limit_bytes=56 * 1024 * 1024

time: 80.6 us -> 77.7 us (0.964)
  Pallas kernels: 78 us -> 75.1 us
    pallas_call x1, Pallas kernels: 78 us -> 75.1 us  [on_device(): pl.pallas_call(functools.partial(kernel, A, B), out_shape=(jax.ShapeDtype...]
where the time goes in v3:
time: 77.7 us; the launch traced here: 77.6 us
  Pallas kernels  75.1 us (97%)
  local copies, waits for them, and re-layouts  1.78 us (2%)
    pallas_call x1, Pallas kernels, on_device(): pl.pallas_call(functools.partial(kernel, A, B), out_shape=(jax.ShapeDtype...  75.1 us
    unnamed x4, local copies, waits for them, and re-layouts  1.78 us

profile of v3, /device:TPU:0, one launch (start us, length us, event | category | flops | bytes accessed | tf_op | source)
XLA Modules:
  0.0 77.6 jit_solution(18057535486518556439)
XLA Ops:
  0.6 75.1 %shard_map.41 = (f32[1024]{0:T(1024)}, f32[2]{0:T(128)}) custom-call(f32[64,1024]{1,0:T(8,128)} %feat_ref.1, f32[1,1024]{1,0:T(1,128)} %bitcast.1), custom_call_target="tpu_custom_call" | custom-call | tf_op jit(solution)/shard_map/pallas_call | solution.py:382
  75.8 0.0 copy-start
  75.8 1.3 %copy.6 = f32[1024]{0:T(1024)} copy(f32[1024]{0:T(1024)} %get-tuple-element.4) | data formatting | bytes 8192
  77.0 0.0 copy-done
  77.0 0.5 copy.7
Async XLA Ops:
  75.8 1.3 %copy-start = (f32[2]{0:T(128)S(1)}, f32[2]{0:T(128)}, u32[]{:S(2)}) copy-start(f32[2]{0:T(128)} %get-tuple-element.5) | copy-start | bytes 28

commit v4 on v3

--- a/solution.py
+++ b/solution.py
@@ -177,12 +177,11 @@
             at = pl.ds(r * tile, tile)
             if first:
                 payoff = jnp.dot(row_op[row_slot, at], col_op[col_slot], preferred_element_type=f32)
-                wide_t = jnp.tanh(payoff)
-                t = wide_t.astype(bf16)
+                t = jnp.tanh(payoff.astype(bf16))
                 kept[kept_slot, at] = t
             else:
                 t = kept[kept_slot, at]
-                wide_t = t.astype(f32)
+            wide_t = t.astype(f32)
             weighed = jnp.zeros((tile, 128), f32)
             plain = jnp.zeros((tile, 128), f32)
             for k in range(n // 128):

time: 77.7 us -> 80.3 us (1.033)
  Pallas kernels: 75.1 us -> 77.7 us
    pallas_call x1, Pallas kernels: 75.1 us -> 77.7 us  [on_device(): pl.pallas_call(functools.partial(kernel, A, B), out_shape=(jax.ShapeDtype...]
where the time goes in v4:
time: 80.3 us; the launch traced here: 80.1 us
  Pallas kernels  77.7 us (97%)
  local copies, waits for them, and re-layouts  1.78 us (2%)
    pallas_call x1, Pallas kernels, on_device(): pl.pallas_call(functools.partial(kernel, A, B), out_shape=(jax.ShapeDtype...  77.7 us
    unnamed x4, local copies, waits for them, and re-layouts  1.78 us

profile of v4, /device:TPU:0, one launch (start us, length us, event | category | flops | bytes accessed | tf_op | source)
XLA Modules:
  0.0 80.1 jit_solution(2737145384248302642)
XLA Ops:
  0.6 77.7 %shard_map.41 = (f32[1024]{0:T(1024)}, f32[2]{0:T(128)}) custom-call(f32[64,1024]{1,0:T(8,128)} %feat_ref.1, f32[1,1024]{1,0:T(1,128)} %bitcast.1), custom_call_target="tpu_custom_call" | custom-call | tf_op jit(solution)/shard_map/pallas_call | solution.py:381
  78.3 0.0 copy-start
  78.3 1.3 %copy.6 = f32[1024]{0:T(1024)} copy(f32[1024]{0:T(1024)} %get-tuple-element.4) | data formatting | bytes 8192
  79.6 0.0 copy-done
  79.6 0.5 copy.7
Async XLA Ops:
  78.3 1.3 %copy-start = (f32[2]{0:T(128)S(1)}, f32[2]{0:T(128)}, u32[]{:S(2)}) copy-start(f32[2]{0:T(128)} %get-tuple-element.5) | copy-start | bytes 28
